TPU v7x, 256 devices: a whole 4x4x8 slice. The times are simulated.
256 devices in a mesh: tm: 8 (over y, z_hi), height: 4 (over z_lo), tensor: 8 (over x, core).
Axes of the slice: x: 4, y: 4, z: 8 (z_hi: 2, z_lo: 4; z = z_hi * 4 + z_lo), core: 2. Of those that a mesh axis runs over, the one named last changes fastest.
Arguments:
- query: bfloat16 [8, 4, 1, 384, 3072], P('tm', 'height', None, 'tensor'), may hold values from -200 to 200
- keys: bfloat16 [8, 4, 1, 384, 3072], P('tm', 'height', None, 'tensor'), may hold values from -7 to 7
- values: bfloat16 [8, 4, 1, 384, 3072], P('tm', 'height', None, 'tensor'), may hold values from -6 to 6
- cotangent: bfloat16 [8, 4, 1, 384, 3072], P('tm', 'height', None, 'tensor'), may hold values from -6 to 6
- extents: int32 [8, 4, 1, 3], replicated, may hold values from 0 to 1, as said below
Outputs:
- attended: bfloat16 [8, 4, 1, 384, 3072], P('tm', 'height', None, 'tensor')
- query_grad: bfloat16 [8, 4, 1, 384, 3072], P('tm', 'height', None, 'tensor')
- key_grad: bfloat16 [8, 4, 1, 384, 3072], P('tm', 'height', None, 'tensor')
- value_grad: bfloat16 [8, 4, 1, 384, 3072], P('tm', 'height', None, 'tensor')
Inputs may be any that keep to these rules, and one draw needn't show every extreme that they name: `extents`: window half-widths in tiles; the half-width along frames is 1 on every tile, the half-width along rows is 1 on every tile of an even frame index.
All inputs are finite; a program needn't handle non-finite values.
Results may differ from a plain program's by a relative error of at most 0.019.
Values may be sent and summed in bfloat16 or wider, within the bound.
A program may use at most 128 MiB of HBM per device.

v0:
```python
import math

import jax
import jax.numpy as jnp
from jax import lax
from jax.sharding import PartitionSpec as P

HD = 128


def padded(x, sides, width):
    for axis, dim in sides:
        devices, length = (lax.axis_size(axis), x.shape[dim])
        up = [(i, (i + 1) % devices) for i in range(devices - 1)]
        down = [(j, i) for i, j in up]
        last = lax.slice_in_dim(x, length - width, length, axis=dim)
        first = lax.slice_in_dim(x, 0, width, axis=dim)
        before = lax.ppermute(last, axis, up)
        after = lax.ppermute(first, axis, down)
        x = jnp.concatenate([before, x, after], axis=dim)
    return x


def passed_along(block, axis, distance):
    devices = range(lax.axis_size(axis))
    route = [(i - distance, i) for i in devices if i - distance in devices]
    return lax.ppermute(block, axis, route)


def for_sending(x):
    return jax.tree.map(lambda a: a.astype(jnp.bfloat16) if a.dtype == jnp.float32 else a, x)


def positions(t_first, h_first, t_count, h_count, w_count):
    grid_t, grid_h, grid_w = jnp.meshgrid(
        jnp.arange(t_count) + t_first,
        jnp.arange(h_count) + h_first,
        jnp.arange(w_count),
        indexing="ij",
    )
    return jnp.stack([grid_t.ravel(), grid_h.ravel(), grid_w.ravel()], axis=1).astype(jnp.int32)


def in_grid(tile_pos, tiles_t, tiles_h):
    return (
        (tile_pos[:, 0] >= 0)
        & (tile_pos[:, 0] < tiles_t)
        & (tile_pos[:, 1] >= 0)
        & (tile_pos[:, 1] < tiles_h)
    )


def within_reach(query_pos, key_pos, query_window):
    return jnp.all(
        jnp.abs(key_pos[None, :, :] - query_pos[:, None, :]) <= query_window[:, None, :], axis=-1
    )


def pick_head(array, head):
    return lax.dynamic_slice_in_dim(array, head * HD, HD, array.ndim - 1)


def merge_heads(stacked):
    heads_here, tiles, rows, width = stacked.shape
    return jnp.transpose(stacked, (1, 2, 0, 3)).reshape(tiles, rows, heads_here * width)


def attend_head(query_rows, every_key_row, every_value_row, output_gradient, allowed, score_scale):
    scores = (
        jnp.einsum("ncg,mhg->ncmh", query_rows, every_key_row, preferred_element_type=jnp.float32)
        * score_scale
    )
    allowed_rows = allowed[:, None, :, None]
    row_max = jnp.max(jnp.where(allowed_rows, scores, -jnp.inf), axis=(2, 3))
    raw_weights = jnp.where(allowed_rows, jnp.exp(scores - row_max[..., None, None]), 0.0)
    row_sum = jnp.sum(raw_weights, axis=(2, 3))
    prob = raw_weights / row_sum[..., None, None]
    softmax_weight = prob.astype(jnp.bfloat16)
    attended = jnp.einsum(
        "zocy,cym->zom", softmax_weight, every_value_row, preferred_element_type=jnp.float32
    ).astype(jnp.bfloat16)
    row_dot = jnp.sum(output_gradient.astype(jnp.float32) * attended.astype(jnp.float32), axis=-1)
    probability_gradient = jnp.einsum(
        "ncg,mhg->ncmh", output_gradient, every_value_row, preferred_element_type=jnp.float32
    )
    logit_gradient = (prob * (probability_gradient - row_dot[..., None, None])).astype(jnp.bfloat16)
    query_grad = (
        jnp.einsum(
            "zocy,cym->zom", logit_gradient, every_key_row, preferred_element_type=jnp.float32
        )
        * score_scale
    ).astype(jnp.bfloat16)
    return (
        attended,
        query_grad,
        jnp.stack((row_max, row_sum, row_dot)),
        softmax_weight,
        logit_gradient,
    )


def shards(query, keys, values, cotangent, extents):
    score_scale = 1.0 / math.sqrt(HD)
    query_own, keys_own, values_own, grads_own = (
        lax.all_to_all(query, "tensor", split_axis=4, concat_axis=3, tiled=True),
        lax.all_to_all(keys, "tensor", split_axis=4, concat_axis=3, tiled=True),
        lax.all_to_all(values, "tensor", split_axis=4, concat_axis=3, tiled=True),
        lax.all_to_all(cotangent, "tensor", split_axis=4, concat_axis=3, tiled=True),
    )
    t_count, h_count, w_count, tile_rows, local_width = query_own.shape
    heads_here = local_width // HD
    head_list = jnp.arange(heads_here, dtype=jnp.int32)
    tiles_t = t_count * lax.axis_size("tm")
    tiles_h = h_count * lax.axis_size("height")
    t_first = lax.axis_index("tm") * t_count
    h_first = lax.axis_index("height") * h_count
    own_pos = positions(t_first, h_first, t_count, h_count, w_count)
    ext_pos = positions(t_first - 1, h_first - 1, t_count + 2, h_count + 2, w_count)
    ext_inside = in_grid(ext_pos, tiles_t, tiles_h)
    zero_index = jnp.int32(0)
    own_windows = lax.dynamic_slice(
        extents, (t_first, h_first, zero_index, zero_index), (t_count, h_count, w_count, 3)
    ).reshape(-1, 3)
    forward_mask = within_reach(own_pos, ext_pos, own_windows) & ext_inside[None, :]
    grid_own = (t_count, h_count, w_count, tile_rows, local_width)
    query_flat = query_own.reshape(-1, tile_rows, local_width)
    grads_flat = grads_own.reshape(-1, tile_rows, local_width)
    stacked = jnp.stack((keys_own, values_own), axis=4)
    widened = padded(stacked, (("tm", 0), ("height", 1)), 1)
    keys_ext = widened[:, :, :, :, 0, :].reshape(-1, tile_rows, local_width)
    values_ext = widened[:, :, :, :, 1, :].reshape(-1, tile_rows, local_width)

    def forward_head(head):
        head_query_rows = pick_head(query_flat, head)
        head_output_gradient = pick_head(grads_flat, head)
        attended_h, query_grad_h, unused_s, head_softmax_weight, head_logit_gradient = attend_head(
            head_query_rows,
            pick_head(keys_ext, head),
            pick_head(values_ext, head),
            head_output_gradient,
            forward_mask,
            score_scale,
        )
        key_terms_h = (
            jnp.einsum(
                "ouns,oui->nsi",
                head_logit_gradient,
                head_query_rows,
                preferred_element_type=jnp.float32,
            )
            * score_scale
        )
        value_terms_h = jnp.einsum(
            "ouns,oui->nsi",
            head_softmax_weight,
            head_output_gradient,
            preferred_element_type=jnp.float32,
        )
        return (attended_h, query_grad_h, key_terms_h, value_terms_h)

    attended_all, query_grad_all, key_all, value_all = lax.map(forward_head, head_list)
    attended = merge_heads(attended_all)
    query_grad = merge_heads(query_grad_all)
    ext_shape = (t_count + 2, h_count + 2, w_count, tile_rows, local_width)
    grad_terms = jnp.stack(
        (merge_heads(key_all).reshape(ext_shape), merge_heads(value_all).reshape(ext_shape)), axis=4
    )
    from_below = passed_along(grad_terms[:, 0:1], "height", -1)
    from_above = passed_along(grad_terms[:, h_count + 1 : h_count + 2], "height", 1)
    middle = grad_terms[:, 1 : h_count + 1]
    middle = middle.at[:, h_count - 1 : h_count].add(from_below)
    middle = middle.at[:, 0:1].add(from_above)
    from_later = passed_along(middle[0:1], "tm", -1)
    from_earlier = passed_along(middle[t_count + 1 : t_count + 2], "tm", 1)
    settled = middle[1 : t_count + 1]
    settled = settled.at[t_count - 1 : t_count].add(from_later)
    settled = settled.at[0:1].add(from_earlier)
    key_grad = settled[:, :, :, :, 0, :].astype(jnp.bfloat16)
    value_grad = settled[:, :, :, :, 1, :].astype(jnp.bfloat16)
    attended = attended.reshape(grid_own)
    query_grad = query_grad.reshape(grid_own)
    return (
        lax.all_to_all(
            for_sending(attended), "tensor", split_axis=3, concat_axis=4, tiled=True
        ).astype(attended.dtype),
        lax.all_to_all(
            for_sending(query_grad), "tensor", split_axis=3, concat_axis=4, tiled=True
        ).astype(query_grad.dtype),
        lax.all_to_all(key_grad, "tensor", split_axis=3, concat_axis=4, tiled=True),
        lax.all_to_all(value_grad, "tensor", split_axis=3, concat_axis=4, tiled=True),
    )


def solution(mesh):
    in_specs = (
        P("tm", "height", None, "tensor", None),
        P("tm", "height", None, "tensor", None),
        P("tm", "height", None, "tensor", None),
        P("tm", "height", None, "tensor", None),
        P(),
    )
    out_specs = (
        P("tm", "height", None, "tensor", None),
        P("tm", "height", None, "tensor", None),
        P("tm", "height", None, "tensor", None),
        P("tm", "height", None, "tensor", None),
    )
    return jax.shard_map(shards, mesh=mesh, in_specs=in_specs, out_specs=out_specs, check_vma=False)
```

profile of v0, /device:TPU:120, one launch (start us, length us, event | category | flops | bytes accessed | tf_op | source)
XLA Modules:
  0.0 507.7 jit_solution(5731338263269347790)
XLA Ops:
  0.7 3.5 copy.133
  4.7 17.0 %reduce.18 = bf16[3072,48]{1,0:T(8,128)(2,1)S(1)} reduce(bf16[3072,1,1,1,48]{4,3,2,1,0:T(2,128)(2,1)S(1)} %bitcast.173, bf16[]{:T(256)} %broadcast.357), dimensions={1,2,3}, to_apply=%bitcast.121.reduce_sub_computation | reduce | bytes 589826
  21.6 1.9 reshape.480
  23.5 4.5 all-to-all-start.1
  29.9 17.0 %reduce.17 = bf16[3072,48]{1,0:T(8,128)(2,1)S(1)} reduce(bf16[3072,1,1,1,48]{4,3,2,1,0:T(2,128)(2,1)S(1)} %bitcast.178, bf16[]{:T(256)} %broadcast.357), dimensions={1,2,3}, to_apply=%bitcast.119.reduce_sub_computation | reduce | bytes 589826
  48.8 4.8 all-to-all-start.2
  56.5 4.9 all-to-all-done.2
  64.5 6.4 %collective-permute-start = (bf16[1,1,1,384,2,384]{5,3,4,2,1,0:T(8,128)(2,1)S(1)}, bf16[1,1,1,384,2,384]{5,3,4,2,1,0:T(8,128)(2,1)S(1)}, u32[]{:S(2)}, u32[]{:S(2)}) collective-permute-start(bf16[1,1,1,384,2,384]{5,3,4,2,1,0:T(8,128)(2,1)S(1)} %pad_maximum_fusion.3), channel_id=1, source_target_pairs={{0,32},{32,64},{64,96},{96,128},{128,160},{160,192},{192,224},{1,3... | collective-permute-start | bytes 1769480 | tf_op jit(solution)/shard_map/ppermute | solution.py:18
  70.9 4.2 collective-permute-start.1
  75.2 27.0 %collective-permute-done = bf16[1,1,1,384,2,384]{5,3,4,2,1,0:T(8,128)(2,1)S(1)} collective-permute-done((bf16[1,1,1,384,2,384]{5,3,4,2,1,0:T(8,128)(2,1)S(1)}, bf16[1,1,1,384,2,384]{5,3,4,2,1,0:T(8,128)(2,1)S(1)}, u32[]{:S(2)}, u32[]{:S(2)}) %collective-permute-start) | collective-permute-done | bytes 589856 | tf_op jit(solution)/shard_map/ppermute | solution.py:18
  102.1 6.4 %collective-permute-done.1 = bf16[1,1,1,384,2,384]{5,3,4,2,1,0:T(8,128)(2,1)S(1)} collective-permute-done((bf16[1,1,1,384,2,384]{5,3,4,2,1,0:T(8,128)(2,1)S(1)}, bf16[1,1,1,384,2,384]{5,3,4,2,1,0:T(8,128)(2,1)S(1)}, u32[]{:S(2)}, u32[]{:S(2)}) %collective-permute-start.1) | collective-permute-done | bytes 589856 | tf_op jit(solution)/shard_map/ppermute | solution.py:19
  111.4 17.4 %collective-permute-start.3 = (bf16[3,1,1,384,2,384]{5,3,4,2,1,0:T(8,128)(2,1)}, bf16[3,1,1,384,2,384]{5,3,4,2,1,0:T(8,128)(2,1)}, u32[]{:S(2)}, u32[]{:S(2)}) collective-permute-start(bf16[3,1,1,384,2,384]{5,3,4,2,1,0:T(8,128)(2,1)} %pad_maximum_fusion.2), channel_id=1, source_target_pairs={{8,0},{16,8},{24,16},{9,1},{17,9},{25,17},{10,2},{18,10},{26,18},{... | collective-permute-start | bytes 5308424 | tf_op jit(solution)/shard_map/ppermute | solution.py:19
  130.7 17.0 %reduce.16 = bf16[3072,48]{1,0:T(8,128)(2,1)S(1)} reduce(bf16[3072,1,1,1,48]{4,3,2,1,0:T(2,128)(2,1)S(1)} %bitcast.179, bf16[]{:T(256)} %broadcast.357), dimensions={1,2,3}, to_apply=%bitcast.117.reduce_sub_computation | reduce | bytes 589826
  149.6 3.7 all-to-all-start
  157.9 17.0 %reduce.19 = bf16[3072,48]{1,0:T(8,128)(2,1)S(1)} reduce(bf16[3072,1,1,1,48]{4,3,2,1,0:T(2,128)(2,1)S(1)} %bitcast.180, bf16[]{:T(256)} %broadcast.357), dimensions={1,2,3}, to_apply=%bitcast.123.reduce_sub_computation | reduce | bytes 589826
  177.8 5.2 %all-to-all-start.3 = ((bf16[8,2,9216]{2,1,0:T(2,128)(2,1)}), bf16[8,2,9216]{2,1,0:T(2,128)(2,1)S(1)}, u32[]{:S(2)}, u32[]{:S(2)}) async-start(bf16[8,2,9216]{2,1,0:T(2,128)(2,1)} %reshape.482), calls=%async_computation.3 | async-start | bytes 589824 | tf_op jit(solution)/shard_map/all_to_all | solution.py:108
  186.9 4.0 all-to-all-done.3
  193.9 3.2 pad_maximum_fusion
  197.1 2.9 fusion.42
  199.9 77.6 %while.24 = (s32[]{:T(128)}, bf16[3,1,384,128]{2,3,1,0:T(8,128)(2,1)}, bf16[3,1,384,128]{2,3,0,1:T(8,128)(2,1)}, f32[3,9,384,128]{2,3,0,1:T(8,128)}, f32[3,9,384...) while((s32[]{:T(128)}, ...), condition=%wide.region_5.6_spmd, body=%wide.region_1.5_spmd.sunk | while | flops 2071067520 | bytes 71586072 | solution.py:161
  201.2 2.1 select_reduce_fusion.2
  204.4 2.8 bitcast_dynamic-update-slice_fusion.5
  207.2 3.4 bitcast_dynamic-update-slice_fusion.4
  210.7 4.4 multiply_convert_fusion.2
  215.2 2.1 multiply_bitcast_fusion.2
  217.3 2.8 copy.192
  220.1 2.8 constant_dynamic-update-slice_fusion.5
  222.9 2.1 fusion.67
  227.0 2.1 select_reduce_fusion.2
  230.3 2.8 bitcast_dynamic-update-slice_fusion.5
  233.1 3.4 bitcast_dynamic-update-slice_fusion.4
  236.6 4.4 multiply_convert_fusion.2
  241.0 2.1 multiply_bitcast_fusion.2
  243.2 2.8 copy.192
  245.9 2.8 constant_dynamic-update-slice_fusion.5
  248.8 2.1 fusion.67
  252.9 2.1 select_reduce_fusion.2
  256.1 2.8 bitcast_dynamic-update-slice_fusion.5
  258.9 3.4 bitcast_dynamic-update-slice_fusion.4
  262.4 4.4 multiply_convert_fusion.2
  266.9 2.1 multiply_bitcast_fusion.2
  269.0 2.8 copy.192
  271.8 2.8 constant_dynamic-update-slice_fusion.5
  274.6 2.1 fusion.67
  277.5 3.7 fusion.33
  281.2 3.2 collective-permute-start.4
  285.9 73.7 %collective-permute-done.4 = f32[3,1,1,384,2,384]{3,5,1,0,4,2:T(8,128)S(1)} collective-permute-done((f32[3,1,1,384,2,384]{3,5,1,0,4,2:T(8,128)S(1)}, f32[3,1,1,384,2,384]{3,5,1,0,4,2:T(8,128)S(1)}, u32[]{:S(2)}, u32[]{:S(2)}) %collective-permute-start.4) | collective-permute-done | bytes 3538976 | tf_op jit(solution)/shard_map/ppermute | solution.py:27
  359.6 4.6 collective-permute-done.5
  366.3 9.4 %collective-permute-start.6 = (f32[1,1,1,384,2,384]{3,5,1,0,4,2:T(8,128)}, f32[1,1,1,384,2,384]{3,5,1,0,4,2:T(8,128)}, u32[]{:S(2)}, u32[]{:S(2)}) collective-permute-start(f32[1,1,1,384,2,384]{3,5,1,0,4,2:T(8,128)} %get-tuple-element.244), channel_id=1, source_target_pairs={{32,0},{64,32},{96,64},{128,96},{160,128},{192,160},{224,192},{33,... | collective-permute-start | bytes 3538952 | tf_op jit(solution)/shard_map/ppermute | solution.py:27
  375.6 1.9 collective-permute-start.7
  377.6 2.9 copy.149
  380.4 4.0 reduce.21
  386.2 4.1 all-to-all-start.5
  390.3 2.9 copy.146
  393.1 4.0 reduce.20
  398.9 4.7 all-to-all-start.4
  403.6 23.3 %collective-permute-done.6 = f32[1,1,1,384,2,384]{3,5,1,0,4,2:T(8,128)} collective-permute-done((f32[1,1,1,384,2,384]{3,5,1,0,4,2:T(8,128)}, f32[1,1,1,384,2,384]{3,5,1,0,4,2:T(8,128)}, u32[]{:S(2)}, u32[]{:S(2)}) %collective-permute-start.6) | collective-permute-done | bytes 1179680 | tf_op jit(solution)/shard_map/ppermute | solution.py:27
  426.9 51.2 %collective-permute-done.7 = f32[1,1,1,384,2,384]{3,5,1,0,4,2:T(8,128)} collective-permute-done((f32[1,1,1,384,2,384]{3,5,1,0,4,2:T(8,128)}, f32[1,1,1,384,2,384]{3,5,1,0,4,2:T(8,128)}, u32[]{:S(2)}, u32[]{:S(2)}) %collective-permute-start.7) | collective-permute-done | bytes 1179680 | tf_op jit(solution)/shard_map/ppermute | solution.py:27
  480.7 2.5 reduce.23
  484.0 3.4 all-to-all-start.7
  488.1 2.5 reduce.22
  491.3 3.9 all-to-all-done.7
  495.2 3.4 all-to-all-start.6
  503.6 2.8 all-to-all-done.6
  (128 shorter events, 57.1 us)
Async XLA Ops:
  0.6 176.1 %copy-start = (s32[8,4,1,3]{0,2,3,1:T(1,128)S(1)}, s32[8,4,1,3]{0,2,3,1:T(1,128)}, u32[]{:S(2)}) copy-start(s32[8,4,1,3]{0,2,3,1:T(1,128)} %param.27) | copy-start | bytes 1156
  0.6 27.4 %copy-start.6 = (bf16[1,1,1,48,3072]{4,3,2,1,0:T(8,128)(2,1)S(1)}, bf16[1,1,1,48,3072]{4,3,2,1,0:T(8,128)(2,1)}, u32[]{:S(2)}) copy-start(bf16[1,1,1,48,3072]{4,3,2,1,0:T(8,128)(2,1)} %param.25) | copy-start | bytes 884740
  23.5 25.3 %all-to-all-start.1 = ((bf16[8,2,9216]{2,1,0:T(2,128)(2,1)}), bf16[8,2,9216]{2,1,0:T(2,128)(2,1)S(1)}, u32[]{:S(2)}, u32[]{:S(2)}) async-start(bf16[8,2,9216]{2,1,0:T(2,128)(2,1)} %reshape.480), calls=%async_computation.1 | async-start | bytes 589824 | tf_op jit(solution)/shard_map/all_to_all | solution.py:106
  48.8 12.7 %all-to-all-start.2 = ((bf16[8,2,9216]{2,1,0:T(2,128)(2,1)}), bf16[8,2,9216]{2,1,0:T(2,128)(2,1)S(1)}, u32[]{:S(2)}, u32[]{:S(2)}) async-start(bf16[8,2,9216]{2,1,0:T(2,128)(2,1)} %reshape.478), calls=%async_computation.2 | async-start | bytes 589824 | tf_op jit(solution)/shard_map/all_to_all | solution.py:107
  62.9 66.0 %copy-start.7 = (bf16[1,1,1,48,3072]{4,3,2,1,0:T(8,128)(2,1)S(1)}, bf16[1,1,1,48,3072]{4,3,2,1,0:T(8,128)(2,1)}, u32[]{:S(2)}) copy-start(bf16[1,1,1,48,3072]{4,3,2,1,0:T(8,128)(2,1)} %param.23) | copy-start | bytes 884740
  64.5 37.6 %collective-permute-start = (bf16[1,1,1,384,2,384]{5,3,4,2,1,0:T(8,128)(2,1)S(1)}, bf16[1,1,1,384,2,384]{5,3,4,2,1,0:T(8,128)(2,1)S(1)}, u32[]{:S(2)}, u32[]{:S(2)}) collective-permute-start(bf16[1,1,1,384,2,384]{5,3,4,2,1,0:T(8,128)(2,1)S(1)} %pad_maximum_fusion.3), channel_id=1, source_target_pairs={{0,32},{32,64},{64,96},{96,128},{128,160},{160,192},{192,224},{1,3... | collective-permute-start | bytes 1769480 | tf_op jit(solution)/shard_map/ppermute | solution.py:18
  70.9 37.6 %collective-permute-start.1 = (bf16[1,1,1,384,2,384]{5,3,4,2,1,0:T(8,128)(2,1)S(1)}, bf16[1,1,1,384,2,384]{5,3,4,2,1,0:T(8,128)(2,1)S(1)}, u32[]{:S(2)}, u32[]{:S(2)}) collective-permute-start(bf16[1,1,1,384,2,384]{5,3,4,2,1,0:T(8,128)(2,1)S(1)} %pad_maximum_fusion.3), channel_id=1, source_target_pairs={{32,0},{64,32},{96,64},{128,96},{160,128},{192,160},{224,192},{33,... | collective-permute-start | bytes 1769480 | tf_op jit(solution)/shard_map/ppermute | solution.py:19
  102.1 9.3 %copy-start.3 = (bf16[1,1,1,384,2,384]{5,3,4,2,1,0:T(8,128)(2,1)}, bf16[1,1,1,384,2,384]{5,3,4,2,1,0:T(8,128)(2,1)S(1)}, u32[]{:S(2)}) copy-start(bf16[1,1,1,384,2,384]{5,3,4,2,1,0:T(8,128)(2,1)S(1)} %collective-permute-done) | copy-start | bytes 1769476
  108.5 2.9 copy-start.5
  110.0 46.1 %copy-start.8 = (bf16[1,1,1,48,3072]{4,3,2,1,0:T(8,128)(2,1)S(1)}, bf16[1,1,1,48,3072]{4,3,2,1,0:T(8,128)(2,1)}, u32[]{:S(2)}) copy-start(bf16[1,1,1,48,3072]{4,3,2,1,0:T(8,128)(2,1)} %param.26) | copy-start | bytes 884740
  110.0 83.8 %collective-permute-start.2 = (bf16[3,1,1,384,2,384]{5,3,4,2,1,0:T(8,128)(2,1)}, bf16[3,1,1,384,2,384]{5,3,4,2,1,0:T(8,128)(2,1)}, u32[]{:S(2)}, u32[]{:S(2)}) collective-permute-start(bf16[3,1,1,384,2,384]{5,3,4,2,1,0:T(8,128)(2,1)} %pad_maximum_fusion.2), channel_id=1, source_target_pairs={{0,8},{8,16},{16,24},{1,9},{9,17},{17,25},{2,10},{10,18},{18,26},{... | collective-permute-start | bytes 5308424 | tf_op jit(solution)/shard_map/ppermute | solution.py:18
  111.4 82.4 %collective-permute-start.3 = (bf16[3,1,1,384,2,384]{5,3,4,2,1,0:T(8,128)(2,1)}, bf16[3,1,1,384,2,384]{5,3,4,2,1,0:T(8,128)(2,1)}, u32[]{:S(2)}, u32[]{:S(2)}) collective-permute-start(bf16[3,1,1,384,2,384]{5,3,4,2,1,0:T(8,128)(2,1)} %pad_maximum_fusion.2), channel_id=1, source_target_pairs={{8,0},{16,8},{24,16},{9,1},{17,9},{25,17},{10,2},{18,10},{26,18},{... | collective-permute-start | bytes 5308424 | tf_op jit(solution)/shard_map/ppermute | solution.py:19
  149.6 28.2 %all-to-all-start = ((bf16[8,2,9216]{2,1,0:T(2,128)(2,1)}), bf16[8,2,9216]{2,1,0:T(2,128)(2,1)S(1)}, u32[]{:S(2)}, u32[]{:S(2)}) async-start(bf16[8,2,9216]{2,1,0:T(2,128)(2,1)} %reshape.476), calls=%async_computation | async-start | bytes 589824 | tf_op jit(solution)/shard_map/all_to_all | solution.py:105
  177.8 13.1 %all-to-all-start.3 = ((bf16[8,2,9216]{2,1,0:T(2,128)(2,1)}), bf16[8,2,9216]{2,1,0:T(2,128)(2,1)S(1)}, u32[]{:S(2)}, u32[]{:S(2)}) async-start(bf16[8,2,9216]{2,1,0:T(2,128)(2,1)} %reshape.482), calls=%async_computation.3 | async-start | bytes 589824 | tf_op jit(solution)/shard_map/all_to_all | solution.py:108
  185.3 8.5 %copy-start.4 = (bf16[1,1,1,384,2,384]{5,3,4,2,1,0:T(8,128)(2,1)S(1)}, bf16[1,1,1,384,2,384]{5,3,4,2,1,0:T(8,128)(2,1)}, u32[]{:S(2)}) copy-start(bf16[1,1,1,384,2,384]{5,3,4,2,1,0:T(8,128)(2,1)} %copy-done.3) | copy-start | bytes 1769476
  203.2 4.0 copy-start.2
  229.1 4.0 copy-start.2
  254.9 3.9 copy-start.2
  277.5 86.7 %slice-start = ((s8[5308416]{0:T(1024)(128)(4,1)}), s8[4194304]{0:T(1024)(128)(4,1)S(1)}, s32[]{:S(2)}) async-start(s8[5308416]{0:T(1024)(128)(4,1)} %bitcast.166), calls=%async_computation.8 | async-start | bytes 8388608
  277.5 86.7 %slice-start.2 = ((s8[5308416]{0:T(1024)(128)(4,1)}), s8[4194304]{0:T(1024)(128)(4,1)S(1)}, s32[]{:S(2)}) async-start(s8[5308416]{0:T(1024)(128)(4,1)} %bitcast.170), calls=%async_computation.10 | async-start | bytes 8388608
  277.5 86.7 %slice-start.1 = ((s8[5308416]{0:T(1024)(128)(4,1)}), s8[1114112]{0:T(1024)(128)(4,1)S(1)}, s32[]{:S(2)}) async-start(s8[5308416]{0:T(1024)(128)(4,1)} %bitcast.166), calls=%async_computation.9 | async-start | bytes 2228224
  277.5 86.7 %slice-start.3 = ((s8[5308416]{0:T(1024)(128)(4,1)}), s8[1114112]{0:T(1024)(128)(4,1)S(1)}, s32[]{:S(2)}) async-start(s8[5308416]{0:T(1024)(128)(4,1)} %bitcast.170), calls=%async_computation.11 | async-start | bytes 2228224
  281.2 78.4 %collective-permute-start.4 = (f32[3,1,1,384,2,384]{3,5,1,0,4,2:T(8,128)S(1)}, f32[3,1,1,384,2,384]{3,5,1,0,4,2:T(8,128)S(1)}, u32[]{:S(2)}, u32[]{:S(2)}) collective-permute-start(f32[3,1,1,384,2,384]{3,5,1,0,4,2:T(8,128)S(1)} %get-tuple-element.240), channel_id=1, source_target_pairs={{8,0},{16,8},{24,16},{9,1},{17,9},{25,17},{10,2},{18,10},{26,18},{... | collective-permute-start | bytes 10616840 | tf_op jit(solution)/shard_map/ppermute | solution.py:27
  284.4 79.7 %collective-permute-start.5 = (f32[3,1,1,384,2,384]{3,5,1,0,4,2:T(8,128)S(1)}, f32[3,1,1,384,2,384]{3,5,1,0,4,2:T(8,128)S(1)}, u32[]{:S(2)}, u32[]{:S(2)}) collective-permute-start(f32[3,1,1,384,2,384]{3,5,1,0,4,2:T(8,128)S(1)} %get-tuple-element.241), channel_id=1, source_target_pairs={{0,8},{8,16},{16,24},{1,9},{9,17},{17,25},{2,10},{10,18},{18,26},{... | collective-permute-start | bytes 10616840 | tf_op jit(solution)/shard_map/ppermute | solution.py:27
  366.3 60.6 %collective-permute-start.6 = (f32[1,1,1,384,2,384]{3,5,1,0,4,2:T(8,128)}, f32[1,1,1,384,2,384]{3,5,1,0,4,2:T(8,128)}, u32[]{:S(2)}, u32[]{:S(2)}) collective-permute-start(f32[1,1,1,384,2,384]{3,5,1,0,4,2:T(8,128)} %get-tuple-element.244), channel_id=1, source_target_pairs={{32,0},{64,32},{96,64},{128,96},{160,128},{192,160},{224,192},{33,... | collective-permute-start | bytes 3538952 | tf_op jit(solution)/shard_map/ppermute | solution.py:27
  375.6 102.5 %collective-permute-start.7 = (f32[1,1,1,384,2,384]{3,5,1,0,4,2:T(8,128)}, f32[1,1,1,384,2,384]{3,5,1,0,4,2:T(8,128)}, u32[]{:S(2)}, u32[]{:S(2)}) collective-permute-start(f32[1,1,1,384,2,384]{3,5,1,0,4,2:T(8,128)} %get-tuple-element.245), channel_id=1, source_target_pairs={{0,32},{32,64},{64,96},{96,128},{128,160},{160,192},{192,224},{1,3... | collective-permute-start | bytes 3538952 | tf_op jit(solution)/shard_map/ppermute | solution.py:27
  386.2 12.7 %all-to-all-start.5 = ((bf16[8,2,9216]{2,1,0:T(2,128)(2,1)}), bf16[8,2,9216]{2,1,0:T(2,128)(2,1)}, u32[]{:S(2)}, u32[]{:S(2)}) async-start(bf16[8,2,9216]{2,1,0:T(2,128)(2,1)} %reshape.486), calls=%async_computation.5 | async-start | bytes 589824 | tf_op jit(solution)/shard_map/all_to_all | solution.py:186
  398.9 85.1 %all-to-all-start.4 = ((bf16[8,2,9216]{2,1,0:T(2,128)(2,1)}), bf16[8,2,9216]{2,1,0:T(2,128)(2,1)}, u32[]{:S(2)}, u32[]{:S(2)}) async-start(bf16[8,2,9216]{2,1,0:T(2,128)(2,1)} %reshape.484), calls=%async_computation.4 | async-start | bytes 589824 | tf_op jit(solution)/shard_map/all_to_all | solution.py:183
  484.0 11.2 %all-to-all-start.7 = ((bf16[8,2,9216]{2,1,0:T(2,128)(2,1)}), bf16[8,2,9216]{2,1,0:T(2,128)(2,1)S(1)}, u32[]{:S(2)}, u32[]{:S(2)}) async-start(bf16[8,2,9216]{2,1,0:T(2,128)(2,1)} %reshape.490), calls=%async_computation.7 | async-start | bytes 589824 | tf_op jit(solution)/shard_map/all_to_all | solution.py:190
  495.2 11.2 %all-to-all-start.6 = ((bf16[8,2,9216]{2,1,0:T(2,128)(2,1)}), bf16[8,2,9216]{2,1,0:T(2,128)(2,1)S(1)}, u32[]{:S(2)}, u32[]{:S(2)}) async-start(bf16[8,2,9216]{2,1,0:T(2,128)(2,1)} %reshape.488), calls=%async_computation.6 | async-start | bytes 589824 | tf_op jit(solution)/shard_map/all_to_all | solution.py:189
  499.9 7.6 %copy-start.1 = (s32[8,4,1,3]{0,2,3,1:T(1,128)S(1)}, s32[8,4,1,3]{0,2,3,1:T(1,128)}, u32[]{:S(2)}) copy-start(s32[8,4,1,3]{0,2,3,1:T(1,128)} %param.27) | copy-start | bytes 1156
where the time goes:
time: 515 us; the launch traced here: 508 us
  waiting for transfers between devices  202 us (39%)
  other arithmetic  98.6 us (19%)
  starting transfers between devices  79.3 us (15%)
  local copies, waits for them, and re-layouts  74.1 us (14%)
  matrix products  50.5 us (10%)
    ppermute x4, waiting for transfers between devices, passed_along(): return lax.ppermute(block, axis, route)  153 us
    unnamed x10, other arithmetic  80.8 us
    unnamed x53, local copies, waits for them, and re-layouts  30.9 us
    ppermute x2, waiting for transfers between devices, padded(): before = lax.ppermute(last, axis, up)  27 us
    ppermute x2, starting transfers between devices, padded(): after = lax.ppermute(first, axis, down)  21.7 us
    dynamic_update_slice x12, local copies, waits for them, and re-layouts, shards(): lax.map(forward_head, head_list)  19.2 us
    ppermute x4, starting transfers between devices, passed_along(): return lax.ppermute(block, axis, route)  16 us
    dot_general x3, matrix products, attend_head(): jnp.einsum('ncg,mhg->ncmh', output_gradient, every_value_row, preferred_e...  13.3 us
  transfers between devices with their start and end apart: 16, of which 10 were waited for; matrix products, arithmetic and copies ran while one was open for 21% of the time, Pallas kernels for 0%

commit v1 on v0

v1 whole, which is shorter than its diff:
```python
import functools
import math

import jax
import jax.numpy as jnp
from jax import lax
from jax.experimental import pallas as pl
from jax.experimental.pallas import tpu as pltpu
from jax.sharding import PartitionSpec as P

MESH = pl.DeviceIdType.MESH
HD = 128
ROWS = 4
FRAMES = 8
NEG = -1e30
BF = jnp.bfloat16
F32 = jnp.float32


def dot(a, b):
    return jnp.dot(a, b, preferred_element_type=F32)


def head_of(x, z):
    low = z % 4
    return 6 * x + 3 * (z // 4) + low - (low > x).astype(jnp.int32)


def place(y, z, x, core):
    return (2 * y + z // 4, z % 4, 2 * x + core)


def kernel(
    tile, chunk,
    ext_ref, q_ref, k_ref, v_ref, g_ref,
    o_att, o_dq, o_dk, o_dv,
    qb, gb, kb, vb, kt, vt, qt, s_all, e_all,
    att_s, dq_s, dk_s, dv_s, dk_acc, dv_acc, dk_ret, dv_ret, dk_got, dv_got,
    in_send, in_recv, halo_send, halo_recv, ret_send, ret_recv, out_send, out_recv,
):
    scale = 1.0 / math.sqrt(HD)
    c2 = scale * math.log2(math.e)
    tm, zlo, ten = (lax.axis_index(a) for a in ("tm", "height", "tensor"))
    y, zhi, x, core = tm // 2, tm % 2, ten // 2, ten % 2
    z = zhi * 4 + zlo
    worker = zlo != x
    frame = 2 * y + core
    mine = worker & (core == zhi)
    has_prev, has_next = frame > 0, frame < FRAMES - 1
    prev_dev = place((frame - 1 + FRAMES) % FRAMES // 2, z, x, 1 - core)
    next_dev = place((frame + 1) % FRAMES // 2, z, x, 1 - core)
    head = head_of(x, z)

    def rows(h):
        return pl.ds(h * tile, tile)

    def source(i):
        return (frame, i // 8, i % 8)

    barrier = pltpu.get_barrier_semaphore()

    def greet(dev):
        pl.semaphore_signal(barrier, inc=1, device_id=dev, device_id_type=MESH)

    @pl.when(worker)
    def _():
        @pl.loop(0, 32)
        def _(i):
            me = (core == zhi) & (i // 8 == zlo) & (i % 8 == ten)

            @pl.when(jnp.logical_not(me))
            def _():
                greet(source(i))

        @pl.when(has_prev)
        def _():
            greet(prev_dev)

        @pl.when(has_next)
        def _():
            greet(next_dev)

    near = has_prev.astype(jnp.int32) + has_next.astype(jnp.int32)
    pl.semaphore_wait(barrier, 24 - mine.astype(jnp.int32) + near * worker.astype(jnp.int32))

    arrays = ((k_ref, kb, 4), (v_ref, vb, 4), (q_ref, qb, 0), (g_ref, gb, 0))

    def put(h):
        return pl.ds(pl.multiple_of(h * tile + ten * chunk, 16), chunk)

    for a, (src, buf, first) in enumerate(arrays):
        @pl.loop(0, 32)
        def _(i, a=a, src=src, buf=buf, first=first):
            x2, z2 = (x + i // 8) % 4, (z + i % 8) % 8
            block = src.at[:, pl.ds(pl.multiple_of(head_of(x2, z2) * HD, HD), HD)]
            dst = buf.at[put(first + zlo)]
            sem = in_recv.at[a, zlo]
            me = (i == 0) & (core == zhi)

            @pl.when((z2 % 4 != x2) & me)
            def _():
                pltpu.make_async_copy(block, dst, sem).start()

            @pl.when((z2 % 4 != x2) & jnp.logical_not(me))
            def _():
                pltpu.make_async_remote_copy(
                    block, dst, in_send.at[a], sem, device_id=place(y, z2, x2, zhi), device_id_type=MESH
                ).start()

    def wait_bytes(ref, sem):
        pltpu.make_async_copy(ref, ref, sem).wait()

    def halo(src, dst, send, recv, dev):
        return pltpu.make_async_remote_copy(src, dst, send, recv, device_id=dev, device_id_type=MESH)

    outs = ((att_s, o_att), (dq_s, o_dq), (dk_s, o_dk), (dv_s, o_dv))

    def send_out(a, h):
        stage, out = outs[a]
        cols = pl.ds(pl.multiple_of(head * HD, HD), HD)

        @pl.loop(0, 8)
        def _(i):
            src = stage.at[pl.ds(pl.multiple_of(h * tile + i * chunk, 16), chunk)]
            dst = out.at[:, cols]
            me = (core == zhi) & (zlo == h) & (i == ten)

            @pl.when(me)
            def _():
                pltpu.make_async_copy(src, dst, out_recv.at[a]).start()

            @pl.when(jnp.logical_not(me))
            def _():
                pltpu.make_async_remote_copy(
                    src, dst, out_send.at[a], out_recv.at[a], device_id=(frame, h, i), device_id_type=MESH
                ).start()

    sides = ((0, has_prev, prev_dev), (1, has_next, next_dev))

    def key_frames(h0, n, fn):
        pass

    @pl.when(worker)
    def _():
        for side, has, dev in sides:
            @pl.when(jnp.logical_not(has))
            def _(side=side):
                here = pl.ds(side * 8 * tile, 4 * tile)
                for ref in (kb, vb):
                    ref[here, :] = jnp.zeros((4 * tile, HD), BF)

        for h in range(ROWS):
            for a, buf in enumerate((kb, vb)):
                wait_bytes(buf.at[rows(4 + h)], in_recv.at[a, h])
                for side, has, dev in sides:
                    @pl.when(has)
                    def _(side=side, dev=dev, a=a, buf=buf, h=h):
                        there = 2 - 2 * side
                        halo(
                            buf.at[rows(4 + h)], buf.at[rows(4 * there + h)],
                            halo_send.at[side, a], halo_recv.at[1 - side, a, h], dev,
                        ).start()

        dk_acc[...] = jnp.zeros_like(dk_acc)
        dv_acc[...] = jnp.zeros_like(dv_acc)

        def turn(f, h):
            r = rows(4 * f + h)
            kt[:, r] = kb[r, :].T
            vt[:, r] = vb[r, :].T

        for h in range(ROWS):
            turn(1, h)
        for h in range(ROWS):
            for side, has, dev in sides:
                @pl.when(has)
                def _(side=side, h=h):
                    for a, buf in enumerate((kb, vb)):
                        wait_bytes(buf.at[rows(8 * side + h)], halo_recv.at[side, a, h])
                turn(2 * side, h)

        for h in range(ROWS):
            lo, hi = max(h - 1, 0), min(h + 1, ROWS - 1)
            count = hi - lo + 1
            reach_t, reach_h = ext_ref[(frame * ROWS + h) * 3], ext_ref[(frame * ROWS + h) * 3 + 1]

            def where_is(j, lo=lo, count=count):
                f, r = j // count, lo + j % count
                return f, r, pl.ds(pl.multiple_of((4 * f + r) * tile, tile), tile)

            wait_bytes(qb.at[rows(h)], in_recv.at[2, h])
            qt[...] = qb[rows(h), :].T

            def scores(j, top, h=h, where_is=where_is, reach_t=reach_t, reach_h=reach_h):
                f, r, at = where_is(j)
                seen = (jnp.abs(f - 1) <= reach_t) & (jnp.abs(r - h) <= reach_h)
                seen &= (f + frame >= 1) & (f + frame <= FRAMES)
                s = dot(kb[at, :], qt[...])
                s = jnp.where(seen, s, NEG)
                s_all[pl.ds(pl.multiple_of(j * tile, tile), tile), :] = s
                return jnp.maximum(top, jnp.max(s.reshape(tile // 8, 8, tile), axis=0))

            top = lax.fori_loop(0, 3 * count, scores, jnp.full((8, tile), NEG, F32))
            top = jnp.max(top, axis=0, keepdims=True)

            def weigh(j, carry, where_is=where_is, top=top):
                total, acc = carry
                f, r, at = where_is(j)
                here = pl.ds(pl.multiple_of(j * tile, tile), tile)
                e = jnp.exp2((s_all[here, :] - top) * c2)
                eb = e.astype(BF)
                e_all[here, :] = eb
                total = total + jnp.sum(e.reshape(tile // 8, 8, tile), axis=0)
                return total, acc + dot(vt[:, at], eb)

            total, acc = lax.fori_loop(
                0, 3 * count, weigh, (jnp.zeros((8, tile), F32), jnp.zeros((HD, tile), F32))
            )
            inverse = 1.0 / jnp.sum(total, axis=0, keepdims=True)
            att = (acc * inverse).astype(BF)
            att_s[rows(h), :] = att.T
            wait_bytes(gb.at[rows(h)], in_recv.at[3, h])
            gt = (gb[rows(h), :].T.astype(F32) * inverse).astype(BF)
            gn = gt.T
            rd = jnp.sum(gt.astype(F32) * att.astype(F32), axis=0, keepdims=True)
            send_out(0, h)
            q = qb[rows(h), :]

            def back(j, acc, where_is=where_is, gt=gt, gn=gn, rd=rd, q=q):
                f, r, at = where_is(j)
                here = pl.ds(pl.multiple_of(j * tile, tile), tile)
                eb = e_all[here, :]
                dp = dot(vb[at, :], gt)
                ds = (eb.astype(F32) * (dp - rd)).astype(BF)
                dv_acc[at, :] += dot(eb, gn)
                dk_acc[at, :] += dot(ds, q)
                return acc + dot(kt[:, at], ds)

            dq = lax.fori_loop(0, 3 * count, back, jnp.zeros((HD, tile), F32))
            dq_s[rows(h), :] = (dq * scale).astype(BF).T
            send_out(1, h)

            done = [h - 1] if h < ROWS - 1 else [h - 1, h]
            for r in [r for r in done if r >= 0]:
                for side, has, dev in sides:
                    @pl.when(has)
                    def _(side=side, dev=dev, r=r):
                        for a, (acc_ref, ret, got, mult) in enumerate(
                            ((dk_acc, dk_ret, dk_got, scale), (dv_acc, dv_ret, dv_got, 1.0))
                        ):
                            ret[rows(4 * side + r), :] = (acc_ref[rows(8 * side + r), :] * mult).astype(BF)
                            halo(
                                ret.at[rows(4 * side + r)], got.at[rows(4 * (1 - side) + r)],
                                ret_send.at[side, a], ret_recv.at[1 - side, a, r], dev,
                            ).start()

        for r in range(ROWS):
            for a, (acc_ref, got, stage, mult) in enumerate(
                ((dk_acc, dk_got, dk_s, scale), (dv_acc, dv_got, dv_s, 1.0))
            ):
                for side, has, dev in sides:
                    @pl.when(has)
                    def _(side=side, a=a, r=r, got=got, acc_ref=acc_ref):
                        there = got.at[rows(4 * side + r)]
                        wait_bytes(there, ret_recv.at[side, a, r])
                        acc_ref[rows(4 + r), :] += there[...].astype(F32) * (1.0 / mult)
                stage[rows(r), :] = (acc_ref[rows(4 + r), :] * mult).astype(BF)
                send_out(2 + a, r)

        for side, has, dev in sides:
            @pl.when(has)
            def _(side=side):
                for a in range(2):
                    wait_bytes(kb.at[pl.ds(0, 4 * tile)], halo_send.at[side, a])
                    wait_bytes(dk_ret.at[pl.ds(0, 4 * tile)], ret_send.at[side, a])

        for a in range(4):
            @pl.when(core == zhi)
            def _(a=a):
                wait_bytes(att_s.at[pl.ds(0, 31 * chunk)], out_send.at[a])

            @pl.when(core != zhi)
            def _(a=a):
                wait_bytes(att_s, out_send.at[a])

    for a in range(4):
        @pl.when(mine)
        def _(a=a):
            wait_bytes(q_ref.at[:, pl.ds(0, 23 * HD)], in_send.at[a])

        @pl.when(jnp.logical_not(mine))
        def _(a=a):
            wait_bytes(q_ref, in_send.at[a])

    for a, (_, out) in enumerate(outs):
        wait_bytes(out, out_recv.at[a])


def solution(mesh):
    spec = P("tm", "height", None, "tensor", None)

    def shards(query, keys, values, cotangent, extents):
        shape = query.shape
        chunk, width = shape[3], shape[4]
        tile = chunk * mesh.shape["tensor"]
        flat = [a.reshape(chunk, width) for a in (query, keys, values, cotangent)]
        any_spec = pl.BlockSpec(memory_space=pl.ANY)
        frame_rows = ROWS * tile
        dma = pltpu.SemaphoreType.DMA
        outs = pl.pallas_call(
            functools.partial(kernel, tile, chunk),
            out_shape=[jax.ShapeDtypeStruct((chunk, width), BF)] * 4,
            in_specs=[pl.BlockSpec(memory_space=pltpu.SMEM)] + [any_spec] * 4,
            out_specs=[any_spec] * 4,
            scratch_shapes=[
                pltpu.VMEM((frame_rows, HD), BF),
                pltpu.VMEM((frame_rows, HD), BF),
                pltpu.VMEM((3 * frame_rows, HD), BF),
                pltpu.VMEM((3 * frame_rows, HD), BF),
                pltpu.VMEM((HD, 3 * frame_rows), BF),
                pltpu.VMEM((HD, 3 * frame_rows), BF),
                pltpu.VMEM((HD, tile), BF),
                pltpu.VMEM((9 * tile, tile), F32),
                pltpu.VMEM((9 * tile, tile), BF),
                *[pltpu.VMEM((frame_rows, HD), BF)] * 4,
                *[pltpu.VMEM((3 * frame_rows, HD), F32)] * 2,
                *[pltpu.VMEM((2 * frame_rows, HD), BF)] * 4,
                dma((4,)), dma((4, 4)), dma((2, 2)), dma((2, 2, 4)),
                dma((2, 2)), dma((2, 2, 4)), dma((4,)), dma((4,)),
            ],
            compiler_params=pltpu.CompilerParams(
                collective_id=0, has_side_effects=True, vmem_limit_bytes=56 * 2**20
            ),
            name="attention",
        )(extents.reshape(-1), *flat)
        return tuple(o.reshape(shape) for o in outs)

    return jax.shard_map(
        shards, mesh=mesh, in_specs=(spec, spec, spec, spec, P()), out_specs=(spec,) * 4, check_vma=False
    )
```

time: 515 us -> 101 us (0.20)
  the two profiles are of different devices: /device:TPU:120 before, /device:TPU:65 now
where the time goes in v1:
time: 101 us; the launch traced here: 100 us
  Pallas kernels  93.8 us (93%)
  local copies, waits for them, and re-layouts  6.01 us (6%)
    pallas_call x1, Pallas kernels, shards(): pl.pallas_call(functools.partial(kernel, tile, chunk), out_shape=[jax.Sha...  93.8 us
    unnamed x13, local copies, waits for them, and re-layouts  5.38 us

profile of v1, /device:TPU:65, one launch (start us, length us, event | category | flops | bytes accessed | tf_op | source)
XLA Modules:
  0.0 100.4 jit_solution(1352072232110205672)
XLA Ops:
  0.6 0.0 copy-start.3
  0.6 0.7 copy-done.3
  1.3 0.1 copy.10
  1.4 0.6 reshape.35.ext_ref
  2.1 93.8 %attention.1 = (bf16[48,3072]{1,0:T(8,128)(2,1)}, bf16[48,3072]{1,0:T(8,128)(2,1)}, bf16[48,3072]{1,0:T(8,128)(2,1)}, bf16[48,3072]{1,0:T(8,128)(2,1)}) custom-call(s32[96]{0:T(128)} %reshape.35.ext_ref, bf16[48,3072]{1,0:T(8,128)(2,1)} %bitcast.14, bf16[48,3072]{1,0:T(8,128)(2,1)} %bitcast.15, bf16[48,3072]{1,0:T(8,128)(2,1)} %bitcast.16, ...), custom_call_target="tpu_custom_call" | custom-call | tf_op jit(solution)/shard_map/attention/pallas_call | solution.py:310
  95.8 0.0 copy-start.2
  95.8 1.7 %copy.15 = bf16[1,1,1,48,3072]{4,3,2,1,0:T(8,128)(2,1)} copy(bf16[1,1,1,48,3072]{4,3,2,1,0:T(8,128)(2,1)} %bitcast.13) | data formatting | bytes 589824
  97.6 0.0 copy-done.2
  97.6 0.0 copy-start.1
  97.6 0.7 copy.16
  98.3 0.4 copy-done.1
  98.7 0.0 copy-start
  98.7 0.7 copy.17
  99.4 0.4 copy-done
  99.7 0.7 copy.18
Async XLA Ops:
  0.6 0.7 copy-start.3
  95.8 1.8 %copy-start.2 = (bf16[48,3072]{1,0:T(8,128)(2,1)S(1)}, bf16[48,3072]{1,0:T(8,128)(2,1)}, u32[]{:S(2)}) copy-start(bf16[48,3072]{1,0:T(8,128)(2,1)} %get-tuple-element.9) | copy-start | bytes 884740
  97.6 1.1 %copy-start.1 = (bf16[48,3072]{1,0:T(8,128)(2,1)S(1)}, bf16[48,3072]{1,0:T(8,128)(2,1)}, u32[]{:S(2)}) copy-start(bf16[48,3072]{1,0:T(8,128)(2,1)} %get-tuple-element.10) | copy-start | bytes 884740
  98.7 1.1 %copy-start = (bf16[48,3072]{1,0:T(8,128)(2,1)S(1)}, bf16[48,3072]{1,0:T(8,128)(2,1)}, u32[]{:S(2)}) copy-start(bf16[48,3072]{1,0:T(8,128)(2,1)} %get-tuple-element.11) | copy-start | bytes 884740

commit v2 on v1

v2 whole, which is shorter than its diff:
```python
import functools
import math

import jax
import jax.numpy as jnp
from jax import lax
from jax.experimental import pallas as pl
from jax.experimental.pallas import tpu as pltpu
from jax.sharding import PartitionSpec as P

MESH = pl.DeviceIdType.MESH
HD = 128
ROWS = 4
FRAMES = 8
LOW = -1e30
HIGH = 1e30
BF = jnp.bfloat16
F32 = jnp.float32


def dot(a, b):
    return jnp.dot(a, b, preferred_element_type=F32)


def head_of(x, z):
    low = z % 4
    return 6 * x + 3 * (z // 4) + low - (low > x).astype(jnp.int32)


def place(y, z, x, core):
    return (2 * y + z // 4, z % 4, 2 * x + core)


def kernel(
    tile, chunk,
    ext_ref, q_ref, k_ref, v_ref, g_ref,
    o_att, o_dq, o_dk, o_dv,
    qb, gb, kb, vb, kt, vt, qt, gt, gn, s_all, e_all, ds_all,
    att_s, dq_s, dk_s, dv_s, dv_own, dk_ret, dv_ret, dk_got, dv_got,
    in_send, in_recv, halo_send, halo_recv, ret_send, ret_recv, out_send, out_recv,
):
    scale = 1.0 / math.sqrt(HD)
    c2 = scale * math.log2(math.e)
    tm, zlo, ten = (lax.axis_index(a) for a in ("tm", "height", "tensor"))
    y, zhi, x, core = tm // 2, tm % 2, ten // 2, ten % 2
    z = zhi * 4 + zlo
    worker = zlo != x
    frame = 2 * y + core
    mine = worker & (core == zhi)
    has_prev, has_next = frame > 0, frame < FRAMES - 1
    prev_dev = place((frame - 1 + FRAMES) % FRAMES // 2, z, x, 1 - core)
    next_dev = place((frame + 1) % FRAMES // 2, z, x, 1 - core)
    sides = ((0, has_prev, prev_dev), (1, has_next, next_dev))
    head = head_of(x, z)

    def rows(first, count=1):
        return pl.ds(first * tile, count * tile)

    def source(i):
        return (frame, i // 8, i % 8)

    barrier = pltpu.get_barrier_semaphore()

    def greet(dev):
        pl.semaphore_signal(barrier, inc=1, device_id=dev, device_id_type=MESH)

    @pl.when(worker)
    def _():
        @pl.loop(0, 32)
        def _(i):
            me = (core == zhi) & (i // 8 == zlo) & (i % 8 == ten)

            @pl.when(jnp.logical_not(me))
            def _():
                greet(source(i))

        for _, has, dev in sides:
            @pl.when(has)
            def _(dev=dev):
                greet(dev)

    near = has_prev.astype(jnp.int32) + has_next.astype(jnp.int32)
    pl.semaphore_wait(barrier, 24 - mine.astype(jnp.int32) + near * worker.astype(jnp.int32))

    K, Q, V, G = range(4)
    arrays = ((k_ref, kb, 4), (q_ref, qb, 0), (v_ref, vb, 4), (g_ref, gb, 0))

    def put(first):
        return pl.ds(pl.multiple_of(first * tile + ten * chunk, 16), chunk)

    for a, (src, buf, first) in enumerate(arrays):
        @pl.loop(0, 32)
        def _(i, a=a, src=src, buf=buf, first=first):
            x2, z2 = (x + i // 8) % 4, (z + i % 8) % 8
            block = src.at[:, pl.ds(pl.multiple_of(head_of(x2, z2) * HD, HD), HD)]
            dst = buf.at[put(first + zlo)]
            sem = in_recv.at[a, zlo]
            me = (i == 0) & (core == zhi)

            @pl.when((z2 % 4 != x2) & me)
            def _():
                pltpu.make_async_copy(block, dst, sem).start()

            @pl.when((z2 % 4 != x2) & jnp.logical_not(me))
            def _():
                pltpu.make_async_remote_copy(
                    block, dst, in_send.at[a], sem, device_id=place(y, z2, x2, zhi), device_id_type=MESH
                ).start()

    def wait_bytes(ref, sem):
        pltpu.make_async_copy(ref, ref, sem).wait()

    outs = ((att_s, o_att), (dq_s, o_dq), (dk_s, o_dk), (dv_s, o_dv))

    def send_out(a, h):
        stage, out = outs[a]
        cols = pl.ds(pl.multiple_of(head * HD, HD), HD)

        @pl.loop(0, 8)
        def _(i):
            src = stage.at[pl.ds(pl.multiple_of(h * tile + i * chunk, 16), chunk)]
            dst = out.at[:, cols]
            me = (core == zhi) & (zlo == h) & (i == ten)

            @pl.when(me)
            def _():
                pltpu.make_async_copy(src, dst, out_recv.at[a]).start()

            @pl.when(jnp.logical_not(me))
            def _():
                pltpu.make_async_remote_copy(
                    src, dst, out_send.at[a], out_recv.at[a], device_id=(frame, h, i), device_id_type=MESH
                ).start()

    def forward(a, buf, h):
        for side, has, dev in sides:
            @pl.when(has)
            def _(side=side, dev=dev):
                there = 2 - 2 * side
                pltpu.make_async_remote_copy(
                    buf.at[rows(4 + h)], buf.at[rows(4 * there + h)],
                    halo_send.at[side, a], halo_recv.at[1 - side, a, h], device_id=dev, device_id_type=MESH,
                ).start()

    def give_back(a, ret, got, r):
        for side, has, dev in sides:
            @pl.when(has)
            def _(side=side, dev=dev):
                pltpu.make_async_remote_copy(
                    ret.at[rows(4 * side + r)], got.at[rows(4 * (1 - side) + r)],
                    ret_send.at[side, a], ret_recv.at[1 - side, a, r], device_id=dev, device_id_type=MESH,
                ).start()

    def near_rows(h):
        lo, hi = max(h - 1, 0), min(h + 1, ROWS - 1)
        return lo, hi - lo + 1

    def pairs(h):
        lo, count = near_rows(h)
        return [(f, r) for f in range(3) for r in range(lo, lo + count)]

    def lanes(h, count=1):
        return pl.ds(h * tile, count * tile)

    def seen(h, f, r):
        reach_t, reach_h = ext_ref[h, 0, 0, frame], ext_ref[h, 1, 0, frame]
        inside = (f + frame >= 1) & (f + frame <= FRAMES)
        return inside & (abs(f - 1) <= reach_t) & (abs(r - h) <= reach_h)

    def over_rows(a, fn):
        return fn(a.reshape(tile // 8, 8, tile), axis=0)

    @pl.when(worker)
    def _():
        for side, has, _ in sides:
            @pl.when(jnp.logical_not(has))
            def _(side=side):
                for ref in (kb, vb):
                    ref[rows(8 * side, 4), :] = jnp.zeros((4 * tile, HD), BF)

        for h in range(ROWS):
            wait_bytes(kb.at[rows(4 + h)], in_recv.at[K, h])
            forward(0, kb, h)
        for h in range(ROWS):
            wait_bytes(qb.at[rows(h)], in_recv.at[Q, h])
            qt[:, lanes(h)] = qb[rows(h), :].T
        for side, has, _ in sides:
            @pl.when(has)
            def _(side=side):
                for h in range(ROWS):
                    wait_bytes(kb.at[rows(8 * side + h)], halo_recv.at[side, 0, h])

        inverse = []
        for h in range(ROWS):
            top = jnp.full((8, tile), LOW, F32)
            for f, r in pairs(h):
                s = dot(kb[rows(4 * f + r), :], qt[:, lanes(h)])
                s_all[rows(4 * f + r), :] = s
                top = jnp.maximum(top, jnp.where(seen(h, f, r), over_rows(s, jnp.max), LOW))
            top = jnp.max(top, axis=0, keepdims=True)
            total = jnp.zeros((8, tile), F32)
            for f, r in pairs(h):
                e = jnp.exp2((s_all[rows(4 * f + r), :] - jnp.where(seen(h, f, r), top, HIGH)) * c2)
                e_all[rows(4 * f + r), lanes(h)] = e.astype(BF)
                total = total + over_rows(e, jnp.sum)
            inverse.append(1.0 / jnp.sum(total, axis=0, keepdims=True))

        for h in range(ROWS):
            wait_bytes(vb.at[rows(4 + h)], in_recv.at[V, h])
            forward(1, vb, h)

        def turn(f):
            for h in range(ROWS):
                r = rows(4 * f + h)
                kt[:, r] = kb[r, :].T
                vt[:, r] = vb[r, :].T

        turn(1)
        for side, has, _ in sides:
            @pl.when(has)
            def _(side=side):
                for h in range(ROWS):
                    wait_bytes(vb.at[rows(8 * side + h)], halo_recv.at[side, 1, h])
            turn(2 * side)

        def across(left, right, h):
            lo, count = near_rows(h)
            return sum(
                dot(left[:, rows(4 * f + lo, count)], right[rows(4 * f + lo, count), lanes(h)]) for f in range(3)
            )

        atts = []
        for h in range(ROWS):
            att = (across(vt, e_all, h) * inverse[h]).astype(BF)
            atts.append(att)
            att_s[rows(h), :] = att.T
            send_out(0, h)

        dots = []
        for h in range(ROWS):
            wait_bytes(gb.at[rows(h)], in_recv.at[G, h])
            g = (gb[rows(h), :].T.astype(F32) * inverse[h]).astype(BF)
            gt[:, lanes(h)] = g
            gn[rows(h), :] = g.T
            dots.append(jnp.sum(g.astype(F32) * atts[h].astype(F32), axis=0, keepdims=True))

        def key_term(left, right, f, r):
            lo, count = near_rows(r)
            return dot(left[rows(4 * f + r), lanes(lo, count)], right[rows(lo, count), :])

        for r in range(ROWS):
            for side in range(2):
                dv_ret[rows(4 * side + r), :] = key_term(e_all, gn, 2 * side, r).astype(BF)
            give_back(1, dv_ret, dv_got, r)
        for r in range(ROWS):
            dv_own[rows(r), :] = key_term(e_all, gn, 1, r)

        for h in range(ROWS):
            for f, r in pairs(h):
                dp = dot(vb[rows(4 * f + r), :], gt[:, lanes(h)])
                e = e_all[rows(4 * f + r), lanes(h)].astype(F32)
                ds_all[rows(4 * f + r), lanes(h)] = (e * (dp - dots[h])).astype(BF)
            dq_s[rows(h), :] = (across(kt, ds_all, h) * scale).astype(BF).T
            send_out(1, h)

        for r in range(ROWS):
            for side in range(2):
                dk_ret[rows(4 * side + r), :] = (key_term(ds_all, qb, 2 * side, r) * scale).astype(BF)
            give_back(0, dk_ret, dk_got, r)

        def returned(a, got, r):
            for side, has, _ in sides:
                @pl.when(has)
                def _(side=side):
                    wait_bytes(got.at[rows(4 * side + r)], ret_recv.at[side, a, r])
            return [
                jnp.where(has, got[rows(4 * side + r), :].astype(F32), 0.0) for side, has, _ in sides
            ]

        for r in range(ROWS):
            a, b = returned(1, dv_got, r)
            dv_s[rows(r), :] = (dv_own[rows(r), :] + a + b).astype(BF)
            send_out(3, r)
        for r in range(ROWS):
            own = key_term(ds_all, qb, 1, r) * scale
            a, b = returned(0, dk_got, r)
            dk_s[rows(r), :] = (own + a + b).astype(BF)
            send_out(2, r)

        for side, has, _ in sides:
            @pl.when(has)
            def _(side=side):
                for a in range(2):
                    wait_bytes(kb.at[rows(0, 4)], halo_send.at[side, a])
                    wait_bytes(dk_ret.at[rows(0, 4)], ret_send.at[side, a])

        for a in range(4):
            @pl.when(core == zhi)
            def _(a=a):
                wait_bytes(att_s.at[pl.ds(0, 31 * chunk)], out_send.at[a])

            @pl.when(core != zhi)
            def _(a=a):
                wait_bytes(att_s, out_send.at[a])

    for a in range(4):
        @pl.when(mine)
        def _(a=a):
            wait_bytes(q_ref.at[:, pl.ds(0, 23 * HD)], in_send.at[a])

        @pl.when(jnp.logical_not(mine))
        def _(a=a):
            wait_bytes(q_ref, in_send.at[a])

    for a, (_, out) in enumerate(outs):
        wait_bytes(out, out_recv.at[a])


def settle(*refs):
    for a, b in zip(refs[:4], refs[4:]):
        b[...] = a[...]


def solution(mesh):
    spec = P("tm", "height", None, "tensor", None)

    def shards(query, keys, values, cotangent, extents):
        shape = query.shape
        chunk, width = shape[3], shape[4]
        tile = chunk * mesh.shape["tensor"]
        flat = [a.reshape(chunk, width) for a in (query, keys, values, cotangent)]
        any_spec = pl.BlockSpec(memory_space=pl.ANY)
        four = ROWS * tile
        dma = pltpu.SemaphoreType.DMA
        pieces = [jax.ShapeDtypeStruct((chunk, width), BF)] * 4
        outs = pl.pallas_call(
            functools.partial(kernel, tile, chunk),
            out_shape=pieces,
            in_specs=[pl.BlockSpec(memory_space=pltpu.SMEM)] + [any_spec] * 4,
            out_specs=[any_spec] * 4,
            scratch_shapes=[
                *[pltpu.VMEM((four, HD), BF)] * 2,
                *[pltpu.VMEM((3 * four, HD), BF)] * 2,
                *[pltpu.VMEM((HD, 3 * four), BF)] * 2,
                *[pltpu.VMEM((HD, four), BF)] * 2,
                pltpu.VMEM((four, HD), BF),
                pltpu.VMEM((3 * four, tile), F32),
                *[pltpu.VMEM((3 * four, four), BF)] * 2,
                *[pltpu.VMEM((four, HD), BF)] * 4,
                pltpu.VMEM((four, HD), F32),
                *[pltpu.VMEM((2 * four, HD), BF)] * 4,
                dma((4,)), dma((4, 4)), dma((2, 2)), dma((2, 2, 4)),
                dma((2, 2)), dma((2, 2, 4)), dma((4,)), dma((4,)),
            ],
            compiler_params=pltpu.CompilerParams(
                collective_id=0, has_side_effects=True, vmem_limit_bytes=58 * 2**20
            ),
            name="attention",
        )(jnp.transpose(extents, (1, 3, 2, 0)), *flat)
        outs = pl.pallas_call(settle, out_shape=pieces, name="settle")(*outs)
        return tuple(o.reshape(shape) for o in outs)

    return jax.shard_map(
        shards, mesh=mesh, in_specs=(spec, spec, spec, spec, P()), out_specs=(spec,) * 4, check_vma=False
    )
```

time: 101 us -> 82.4 us (0.82)
  the two profiles are of different devices: /device:TPU:65 before, /device:TPU:81 now
where the time goes in v2:
time: 82.4 us; the launch traced here: 82.2 us
  Pallas kernels  81.6 us (99%)
    pallas_call x1, Pallas kernels, shards(): pl.pallas_call(functools.partial(kernel, tile, chunk), out_shape=pieces,...  79.3 us
    pallas_call x1, Pallas kernels, shards(): outs = pl.pallas_call(settle, out_shape=pieces, name='settle')(*outs)  2.26 us

profile of v2, /device:TPU:81, one launch (start us, length us, event | category | flops | bytes accessed | tf_op | source)
XLA Modules:
  0.0 82.2 jit_solution(10883324215699306535)
XLA Ops:
  0.6 79.3 %attention.1 = (bf16[48,3072]{1,0:T(8,128)(2,1)}, bf16[48,3072]{1,0:T(8,128)(2,1)}, bf16[48,3072]{1,0:T(8,128)(2,1)}, bf16[48,3072]{1,0:T(8,128)(2,1)}) custom-call(s32[4,3,1,8]{3,2,1,0:T(1,128)} %bitcast.13, bf16[48,3072]{1,0:T(8,128)(2,1)} %bitcast.9, bf16[48,3072]{1,0:T(8,128)(2,1)} %bitcast.10, bf16[48,3072]{1,0:T(8,128)(2,1)} %bitcast.11, ...), custom_call_target="tpu_custom_call" | custom-call | tf_op jit(solution)/shard_map/attention/pallas_call | solution.py:336
  80.0 2.3 %settle.1 = (bf16[48,3072]{1,0:T(8,128)(2,1)}, bf16[48,3072]{1,0:T(8,128)(2,1)}, bf16[48,3072]{1,0:T(8,128)(2,1)}, bf16[48,3072]{1,0:T(8,128)(2,1)}) custom-call(bf16[48,3072]{1,0:T(8,128)(2,1)} %get-tuple-element.12.refs_0_, bf16[48,3072]{1,0:T(8,128)(2,1)} %get-tuple-element.13.refs_1_, bf16[48,3072]{1,0:T(8,128)(2,1)} %get-tuple-element.14.refs_2_, ...), custom_call_target="tpu_custom_call" | custom-call | tf_op jit(solution)/shard_map/settle/pallas_call | solution.py:360

commit v3 on v2

--- a/solution.py
+++ b/solution.py
@@ -36,8 +36,9 @@
     ext_ref, q_ref, k_ref, v_ref, g_ref,
     o_att, o_dq, o_dk, o_dv,
     qb, gb, kb, vb, kt, vt, qt, gt, gn, s_all, e_all, ds_all,
-    att_s, dq_s, dk_s, dv_s, dv_own, dk_ret, dv_ret, dk_got, dv_got,
-    in_send, in_recv, halo_send, halo_recv, ret_send, ret_recv, out_send, out_recv,
+    att_s, dq_s, dk_s, dv_s, dk_ret, dv_ret, dk_got, dv_got,
+    relay_buf,
+    in_send, in_recv, halo_send, halo_recv, ret_send, ret_recv, out_send, out_recv, relay_recv,
 ):
     scale = 1.0 / math.sqrt(HD)
     c2 = scale * math.log2(math.e)
@@ -79,8 +80,23 @@
             def _(dev=dev):
                 greet(dev)
 
-    near = has_prev.astype(jnp.int32) + has_next.astype(jnp.int32)
-    pl.semaphore_wait(barrier, 24 - mine.astype(jnp.int32) + near * worker.astype(jnp.int32))
+    relay_dev = place(y, z, zlo, core)
+    own_relay = jnp.logical_not(worker) & (core == zhi)
+    for zh in range(2):
+        @pl.when(jnp.logical_not(own_relay & (zhi == zh)))
+        def _(zh=zh):
+            greet((2 * y + zh, x, 2 * x + zhi))
+
+    @pl.when(jnp.logical_not(worker))
+    def _():
+        for step in range(1, 4):
+            greet(place(y, z, (x + step) % 4, core))
+
+    def number(flag):
+        return flag.astype(jnp.int32)
+
+    greetings = jnp.where(worker, 25 - number(mine) + number(has_prev) + number(has_next), 32 - number(own_relay))
+    pl.semaphore_wait(barrier, greetings)
 
     K, Q, V, G = range(4)
     arrays = ((k_ref, kb, 4), (q_ref, qb, 0), (v_ref, vb, 4), (g_ref, gb, 0))
@@ -94,7 +110,7 @@
             x2, z2 = (x + i // 8) % 4, (z + i % 8) % 8
             block = src.at[:, pl.ds(pl.multiple_of(head_of(x2, z2) * HD, HD), HD)]
             dst = buf.at[put(first + zlo)]
-            sem = in_recv.at[a, zlo]
+            sem = in_recv.at[a, i // 8]
             me = (i == 0) & (core == zhi)
 
             @pl.when((z2 % 4 != x2) & me)
@@ -112,35 +128,90 @@
 
     outs = ((att_s, o_att), (dq_s, o_dq), (dk_s, o_dk), (dv_s, o_dv))
 
-    def send_out(a, h):
+    def columns(which):
+        return pl.ds(pl.multiple_of(which * HD, HD), HD)
+
+    def slot(a, who, h):
+        return pl.ds(pl.multiple_of(((a * 4 + who) * ROWS + h) * 2 * chunk, 16), 2 * chunk)
+
+    def send_out(a, row=None):
         stage, out = outs[a]
-        cols = pl.ds(pl.multiple_of(head * HD, HD), HD)
-
-        @pl.loop(0, 8)
+        count = ROWS if row is None else 1
+
+        def which(i):
+            return (i + zlo) % ROWS if row is None else row
+
+        @pl.loop(0, count)
         def _(i):
-            src = stage.at[pl.ds(pl.multiple_of(h * tile + i * chunk, 16), chunk)]
-            dst = out.at[:, cols]
-            me = (core == zhi) & (zlo == h) & (i == ten)
+            h = which(i)
+            first = pl.multiple_of(h * tile + 2 * zlo * chunk, 16)
+            pltpu.make_async_remote_copy(
+                stage.at[pl.ds(first, 2 * chunk)], relay_buf.at[slot(a, x, h)], out_send.at[a],
+                relay_recv.at[a, x, h], device_id=relay_dev, device_id_type=MESH,
+            ).start()
+
+        @pl.loop(0, 6 * count)
+        def _(i):
+            h, piece = which(i // 6), (2 * zlo + 2 + i % 6) % 8
+            first = pl.multiple_of(h * tile + piece * chunk, 16)
+            me = (core == zhi) & (zlo == h) & (piece == ten)
 
             @pl.when(me)
             def _():
-                pltpu.make_async_copy(src, dst, out_recv.at[a]).start()
+                pltpu.make_async_copy(stage.at[pl.ds(first, chunk)], out.at[:, columns(head)], out_recv.at[a]).start()
 
             @pl.when(jnp.logical_not(me))
             def _():
                 pltpu.make_async_remote_copy(
-                    src, dst, out_send.at[a], out_recv.at[a], device_id=(frame, h, i), device_id_type=MESH
+                    stage.at[pl.ds(first, chunk)], out.at[:, columns(head)], out_send.at[a], out_recv.at[a],
+                    device_id=(frame, h, piece), device_id_type=MESH,
                 ).start()
 
-    def forward(a, buf, h):
+    def pass_on(a):
+        _, out = outs[a]
+
+        @pl.loop(0, 12)
+        def _(i):
+            h, who = (i // 3 + (zlo if a > 1 else 0)) % ROWS, (x + 1 + i % 3) % 4
+            wait_bytes(relay_buf.at[slot(a, who, h)], relay_recv.at[a, who, h])
+            base = pl.multiple_of(((a * 4 + who) * ROWS + h) * 2 * chunk, 16)
+            cols = columns(head_of(who, z))
+            for s in range(2):
+                src = relay_buf.at[pl.ds(base + s * chunk, chunk)]
+                me = (core == zhi) & (h == zlo) & (core == s)
+
+                @pl.when(me)
+                def _(src=src):
+                    pltpu.make_async_copy(src, out.at[:, cols], out_recv.at[a]).start()
+
+                @pl.when(jnp.logical_not(me))
+                def _(src=src, s=s):
+                    pltpu.make_async_remote_copy(
+                        src, out.at[:, cols], out_send.at[a], out_recv.at[a],
+                        device_id=(frame, h, 2 * x + s), device_id_type=MESH,
+                    ).start()
+
+    def forward(a, buf, d):
+        piece = (x - d + 4) % 4 * 2 * chunk
         for side, has, dev in sides:
             @pl.when(has)
             def _(side=side, dev=dev):
                 there = 2 - 2 * side
-                pltpu.make_async_remote_copy(
-                    buf.at[rows(4 + h)], buf.at[rows(4 * there + h)],
-                    halo_send.at[side, a], halo_recv.at[1 - side, a, h], device_id=dev, device_id_type=MESH,
-                ).start()
+                for h in range(ROWS):
+                    pltpu.make_async_remote_copy(
+                        buf.at[pl.ds(pl.multiple_of((4 + h) * tile + piece, 16), 2 * chunk)],
+                        buf.at[pl.ds(pl.multiple_of((4 * there + h) * tile + piece, 16), 2 * chunk)],
+                        halo_send.at[side, a], halo_recv.at[1 - side, a], device_id=dev, device_id_type=MESH,
+                    ).start()
+
+    def arrived(a, d):
+        wait_bytes(qb.at[rows(0)], in_recv.at[a, d])
+
+    def halo_arrived(a, buf):
+        for side, has, _ in sides:
+            @pl.when(has)
+            def _(side=side):
+                wait_bytes(buf.at[rows(8 * side, 4)], halo_recv.at[side, a])
 
     def give_back(a, ret, got, r):
         for side, has, dev in sides:
@@ -178,17 +249,14 @@
                 for ref in (kb, vb):
                     ref[rows(8 * side, 4), :] = jnp.zeros((4 * tile, HD), BF)
 
+        for d in range(4):
+            arrived(K, d)
+            forward(0, kb, d)
+        for d in range(4):
+            arrived(Q, d)
         for h in range(ROWS):
-            wait_bytes(kb.at[rows(4 + h)], in_recv.at[K, h])
-            forward(0, kb, h)
-        for h in range(ROWS):
-            wait_bytes(qb.at[rows(h)], in_recv.at[Q, h])
             qt[:, lanes(h)] = qb[rows(h), :].T
-        for side, has, _ in sides:
-            @pl.when(has)
-            def _(side=side):
-                for h in range(ROWS):
-                    wait_bytes(kb.at[rows(8 * side + h)], halo_recv.at[side, 0, h])
+        halo_arrived(0, kb)
 
         inverse = []
         for h in range(ROWS):
@@ -205,23 +273,21 @@
                 total = total + over_rows(e, jnp.sum)
             inverse.append(1.0 / jnp.sum(total, axis=0, keepdims=True))
 
-        for h in range(ROWS):
-            wait_bytes(vb.at[rows(4 + h)], in_recv.at[V, h])
-            forward(1, vb, h)
-
-        def turn(f):
+        for d in range(4):
+            arrived(V, d)
+            forward(1, vb, d)
+
+        def turn(to, buf, f):
             for h in range(ROWS):
                 r = rows(4 * f + h)
-                kt[:, r] = kb[r, :].T
-                vt[:, r] = vb[r, :].T
-
-        turn(1)
-        for side, has, _ in sides:
-            @pl.when(has)
-            def _(side=side):
-                for h in range(ROWS):
-                    wait_bytes(vb.at[rows(8 * side + h)], halo_recv.at[side, 1, h])
-            turn(2 * side)
+                to[:, r] = buf[r, :].T
+
+        turn(vt, vb, 1)
+        for f in range(3):
+            turn(kt, kb, f)
+        halo_arrived(1, vb)
+        turn(vt, vb, 0)
+        turn(vt, vb, 2)
 
         def across(left, right, h):
             lo, count = near_rows(h)
@@ -237,8 +303,9 @@
             send_out(0, h)
 
         dots = []
+        for d in range(4):
+            arrived(G, d)
         for h in range(ROWS):
-            wait_bytes(gb.at[rows(h)], in_recv.at[G, h])
             g = (gb[rows(h), :].T.astype(F32) * inverse[h]).astype(BF)
             gt[:, lanes(h)] = g
             gn[rows(h), :] = g.T
@@ -252,9 +319,6 @@
             for side in range(2):
                 dv_ret[rows(4 * side + r), :] = key_term(e_all, gn, 2 * side, r).astype(BF)
             give_back(1, dv_ret, dv_got, r)
-        for r in range(ROWS):
-            dv_own[rows(r), :] = key_term(e_all, gn, 1, r)
-
         for h in range(ROWS):
             for f, r in pairs(h):
                 dp = dot(vb[rows(4 * f + r), :], gt[:, lanes(h)])
@@ -279,13 +343,13 @@
 
         for r in range(ROWS):
             a, b = returned(1, dv_got, r)
-            dv_s[rows(r), :] = (dv_own[rows(r), :] + a + b).astype(BF)
-            send_out(3, r)
+            dv_s[rows(r), :] = (key_term(e_all, gn, 1, r) + a + b).astype(BF)
+        send_out(3)
         for r in range(ROWS):
             own = key_term(ds_all, qb, 1, r) * scale
             a, b = returned(0, dk_got, r)
             dk_s[rows(r), :] = (own + a + b).astype(BF)
-            send_out(2, r)
+        send_out(2)
 
         for side, has, _ in sides:
             @pl.when(has)
@@ -302,6 +366,19 @@
             @pl.when(core != zhi)
             def _(a=a):
                 wait_bytes(att_s, out_send.at[a])
+
+    @pl.when(jnp.logical_not(worker))
+    def _():
+        for a in (0, 1, 3, 2):
+            pass_on(a)
+        for a in range(4):
+            @pl.when(core == zhi)
+            def _(a=a):
+                wait_bytes(relay_buf.at[pl.ds(0, 21 * chunk)], out_send.at[a])
+
+            @pl.when(core != zhi)
+            def _(a=a):
+                wait_bytes(relay_buf.at[pl.ds(0, 24 * chunk)], out_send.at[a])
 
     for a in range(4):
         @pl.when(mine)
@@ -347,10 +424,10 @@
                 pltpu.VMEM((3 * four, tile), F32),
                 *[pltpu.VMEM((3 * four, four), BF)] * 2,
                 *[pltpu.VMEM((four, HD), BF)] * 4,
-                pltpu.VMEM((four, HD), F32),
                 *[pltpu.VMEM((2 * four, HD), BF)] * 4,
-                dma((4,)), dma((4, 4)), dma((2, 2)), dma((2, 2, 4)),
-                dma((2, 2)), dma((2, 2, 4)), dma((4,)), dma((4,)),
+                pltpu.VMEM((4 * 4 * ROWS * 2 * chunk, HD), BF),
+                dma((4,)), dma((4, 4)), dma((2, 2)), dma((2, 2)),
+                dma((2, 2)), dma((2, 2, 4)), dma((4,)), dma((4,)), dma((4, 4, ROWS)),
             ],
             compiler_params=pltpu.CompilerParams(
                 collective_id=0, has_side_effects=True, vmem_limit_bytes=58 * 2**20

time: 82.4 us -> 77.7 us (0.943)
  the two profiles are of different devices: /device:TPU:81 before, /device:TPU:1 now
where the time goes in v3:
time: 77.7 us; the launch traced here: 76.8 us
  Pallas kernels  76.2 us (98%)
    pallas_call x1, Pallas kernels, shards(): pl.pallas_call(functools.partial(kernel, tile, chunk), out_shape=pieces,...  73.9 us
    pallas_call x1, Pallas kernels, shards(): outs = pl.pallas_call(settle, out_shape=pieces, name='settle')(*outs)  2.26 us

profile of v3, /device:TPU:1, one launch (start us, length us, event | category | flops | bytes accessed | tf_op | source)
XLA Modules:
  0.0 76.8 jit_solution(5408454932572954448)
XLA Ops:
  0.6 73.9 %attention.1 = (bf16[48,3072]{1,0:T(8,128)(2,1)}, bf16[48,3072]{1,0:T(8,128)(2,1)}, bf16[48,3072]{1,0:T(8,128)(2,1)}, bf16[48,3072]{1,0:T(8,128)(2,1)}) custom-call(s32[4,3,1,8]{3,2,1,0:T(1,128)} %bitcast.13, bf16[48,3072]{1,0:T(8,128)(2,1)} %bitcast.9, bf16[48,3072]{1,0:T(8,128)(2,1)} %bitcast.10, bf16[48,3072]{1,0:T(8,128)(2,1)} %bitcast.11, ...), custom_call_target="tpu_custom_call" | custom-call | tf_op jit(solution)/shard_map/attention/pallas_call | solution.py:413
  74.6 2.3 %settle.1 = (bf16[48,3072]{1,0:T(8,128)(2,1)}, bf16[48,3072]{1,0:T(8,128)(2,1)}, bf16[48,3072]{1,0:T(8,128)(2,1)}, bf16[48,3072]{1,0:T(8,128)(2,1)}) custom-call(bf16[48,3072]{1,0:T(8,128)(2,1)} %get-tuple-element.12.refs_0_, bf16[48,3072]{1,0:T(8,128)(2,1)} %get-tuple-element.13.refs_1_, bf16[48,3072]{1,0:T(8,128)(2,1)} %get-tuple-element.14.refs_2_, ...), custom_call_target="tpu_custom_call" | custom-call | tf_op jit(solution)/shard_map/settle/pallas_call | solution.py:437

commit v4 on v3

--- a/solution.py
+++ b/solution.py
@@ -172,7 +172,7 @@
 
         @pl.loop(0, 12)
         def _(i):
-            h, who = (i // 3 + (zlo if a > 1 else 0)) % ROWS, (x + 1 + i % 3) % 4
+            h, who = i // 3, (x + 1 + i % 3) % 4
             wait_bytes(relay_buf.at[slot(a, who, h)], relay_recv.at[a, who, h])
             base = pl.multiple_of(((a * 4 + who) * ROWS + h) * 2 * chunk, 16)
             cols = columns(head_of(who, z))
@@ -344,12 +344,12 @@
         for r in range(ROWS):
             a, b = returned(1, dv_got, r)
             dv_s[rows(r), :] = (key_term(e_all, gn, 1, r) + a + b).astype(BF)
-        send_out(3)
+            send_out(3, r)
         for r in range(ROWS):
             own = key_term(ds_all, qb, 1, r) * scale
             a, b = returned(0, dk_got, r)
             dk_s[rows(r), :] = (own + a + b).astype(BF)
-        send_out(2)
+            send_out(2, r)
 
         for side, has, _ in sides:
             @pl.when(has)
@@ -394,8 +394,16 @@
 
 
 def settle(*refs):
-    for a, b in zip(refs[:4], refs[4:]):
-        b[...] = a[...]
+    froms, tos, held, loaded, stored = refs[:4], refs[4:8], refs[8:12], refs[12], refs[13]
+    loads = [pltpu.make_async_copy(a, b, loaded.at[i]) for i, (a, b) in enumerate(zip(froms, held))]
+    stores = [pltpu.make_async_copy(a, b, stored.at[i]) for i, (a, b) in enumerate(zip(held, tos))]
+    for load in loads:
+        load.start()
+    for load, store in zip(loads, stores):
+        load.wait()
+        store.start()
+    for store in stores:
+        store.wait()
 
 
 def solution(mesh):
@@ -434,7 +442,15 @@
             ),
             name="attention",
         )(jnp.transpose(extents, (1, 3, 2, 0)), *flat)
-        outs = pl.pallas_call(settle, out_shape=pieces, name="settle")(*outs)
+        outs = pl.pallas_call(
+            settle,
+            out_shape=pieces,
+            in_specs=[any_spec] * 4,
+            out_specs=[any_spec] * 4,
+            scratch_shapes=[*[pltpu.VMEM((chunk, width), BF)] * 4, dma((4,)), dma((4,))],
+            compiler_params=pltpu.CompilerParams(vmem_limit_bytes=58 * 2**20),
+            name="settle",
+        )(*outs)
         return tuple(o.reshape(shape) for o in outs)
 
     return jax.shard_map(

time: 77.7 us -> 77.3 us (level)
  no operation moved by 1% of the time
where the time goes in v4:
time: 77.3 us; the launch traced here: 77.2 us
  Pallas kernels  76.4 us (99%)
  between operations  0.82 us (1%)
    pallas_call x1, Pallas kernels, shards(): pl.pallas_call(functools.partial(kernel, tile, chunk), out_shape=pieces,...  74.3 us
    pallas_call x1, Pallas kernels, shards(): pl.pallas_call(settle, out_shape=pieces, in_specs=[any_spec] * 4, out_spe...  2.04 us

profile of v4, /device:TPU:1, one launch (start us, length us, event | category | flops | bytes accessed | tf_op | source)
XLA Modules:
  0.0 77.2 jit_solution(1174943997249649605)
XLA Ops:
  0.6 74.3 %attention.1 = (bf16[48,3072]{1,0:T(8,128)(2,1)}, bf16[48,3072]{1,0:T(8,128)(2,1)}, bf16[48,3072]{1,0:T(8,128)(2,1)}, bf16[48,3072]{1,0:T(8,128)(2,1)}) custom-call(s32[4,3,1,8]{3,2,1,0:T(1,128)} %bitcast.13, bf16[48,3072]{1,0:T(8,128)(2,1)} %bitcast.9, bf16[48,3072]{1,0:T(8,128)(2,1)} %bitcast.10, bf16[48,3072]{1,0:T(8,128)(2,1)} %bitcast.11, ...), custom_call_target="tpu_custom_call" | custom-call | tf_op jit(solution)/shard_map/attention/pallas_call | solution.py:421
  75.0 2.0 %settle.1 = (bf16[48,3072]{1,0:T(8,128)(2,1)}, bf16[48,3072]{1,0:T(8,128)(2,1)}, bf16[48,3072]{1,0:T(8,128)(2,1)}, bf16[48,3072]{1,0:T(8,128)(2,1)}) custom-call(bf16[48,3072]{1,0:T(8,128)(2,1)} %get-tuple-element.12.refs_0_, bf16[48,3072]{1,0:T(8,128)(2,1)} %get-tuple-element.13.refs_1_, bf16[48,3072]{1,0:T(8,128)(2,1)} %get-tuple-element.14.refs_2_, ...), custom_call_target="tpu_custom_call" | custom-call | tf_op jit(solution)/shard_map/settle/pallas_call | solution.py:445

commit v5 on v4

--- a/solution.py
+++ b/solution.py
@@ -172,7 +172,7 @@
 
         @pl.loop(0, 12)
         def _(i):
-            h, who = i // 3, (x + 1 + i % 3) % 4
+            h, who = (i // 3 + (zlo if a > 1 else 0)) % ROWS, (x + 1 + i % 3) % 4
             wait_bytes(relay_buf.at[slot(a, who, h)], relay_recv.at[a, who, h])
             base = pl.multiple_of(((a * 4 + who) * ROWS + h) * 2 * chunk, 16)
             cols = columns(head_of(who, z))
@@ -344,12 +344,12 @@
         for r in range(ROWS):
             a, b = returned(1, dv_got, r)
             dv_s[rows(r), :] = (key_term(e_all, gn, 1, r) + a + b).astype(BF)
-            send_out(3, r)
+        send_out(3)
         for r in range(ROWS):
             own = key_term(ds_all, qb, 1, r) * scale
             a, b = returned(0, dk_got, r)
             dk_s[rows(r), :] = (own + a + b).astype(BF)
-            send_out(2, r)
+        send_out(2)
 
         for side, has, _ in sides:
             @pl.when(has)

time: 77.3 us -> 77.6 us (level)
  no operation moved by 1% of the time
where the time goes in v5:
time: 77.6 us; the launch traced here: 76.8 us
  Pallas kernels  76 us (98%)
  between operations  0.82 us (1%)
    pallas_call x1, Pallas kernels, shards(): pl.pallas_call(functools.partial(kernel, tile, chunk), out_shape=pieces,...  73.9 us
    pallas_call x1, Pallas kernels, shards(): pl.pallas_call(settle, out_shape=pieces, in_specs=[any_spec] * 4, out_spe...  2.04 us

profile of v5, /device:TPU:1, one launch (start us, length us, event | category | flops | bytes accessed | tf_op | source)
XLA Modules:
  0.0 76.8 jit_solution(2029377739519428048)
XLA Ops:
  0.6 73.9 %attention.1 = (bf16[48,3072]{1,0:T(8,128)(2,1)}, bf16[48,3072]{1,0:T(8,128)(2,1)}, bf16[48,3072]{1,0:T(8,128)(2,1)}, bf16[48,3072]{1,0:T(8,128)(2,1)}) custom-call(s32[4,3,1,8]{3,2,1,0:T(1,128)} %bitcast.13, bf16[48,3072]{1,0:T(8,128)(2,1)} %bitcast.9, bf16[48,3072]{1,0:T(8,128)(2,1)} %bitcast.10, bf16[48,3072]{1,0:T(8,128)(2,1)} %bitcast.11, ...), custom_call_target="tpu_custom_call" | custom-call | tf_op jit(solution)/shard_map/attention/pallas_call | solution.py:421
  74.6 2.0 %settle.1 = (bf16[48,3072]{1,0:T(8,128)(2,1)}, bf16[48,3072]{1,0:T(8,128)(2,1)}, bf16[48,3072]{1,0:T(8,128)(2,1)}, bf16[48,3072]{1,0:T(8,128)(2,1)}) custom-call(bf16[48,3072]{1,0:T(8,128)(2,1)} %get-tuple-element.12.refs_0_, bf16[48,3072]{1,0:T(8,128)(2,1)} %get-tuple-element.13.refs_1_, bf16[48,3072]{1,0:T(8,128)(2,1)} %get-tuple-element.14.refs_2_, ...), custom_call_target="tpu_custom_call" | custom-call | tf_op jit(solution)/shard_map/settle/pallas_call | solution.py:445
